TPU v7x, 32 devices: a whole 2x2x4 slice. The times are simulated.
32 devices in a mesh: design: 2 (over y), cluster: 4 (over z), blk: 2 (over x), sub: 2 (over core).
Axes of the slice: x: 2, y: 2, z: 4, core: 2. Of those that a mesh axis runs over, the one named last changes fastest.
Arguments:
- density: bfloat16 [16, 256, 256], P(('design', 'cluster')), parts along dimension 0, may hold values from -6 to 6
- far_cols: int32 [256], P(('design', 'cluster', 'blk', 'sub')), parts along dimension 0, may hold values from 0 to 1
- far_bucket: int32 [256], P(('design', 'cluster', 'blk', 'sub')), parts along dimension 0, may hold values from 0 to 4
- far_v: bfloat16 [256, 64, 256], P(('design', 'cluster', 'blk', 'sub')), parts along dimension 0, may hold values from -0.375 to 0.375
- far_u: bfloat16 [256, 64, 256], P(('design', 'cluster', 'blk', 'sub')), parts along dimension 0, may hold values from -0.1875 to 0.1875
- near_rows: int32 [64], P(('design', 'cluster', 'blk', 'sub')), parts along dimension 0, may hold values from 0 to 1
- near_cols: int32 [64], P(('design', 'cluster', 'blk', 'sub')), parts along dimension 0, may hold values from 0 to 5
- near_tiles: bfloat16 [64, 256, 256], P(('design', 'cluster', 'blk', 'sub')), parts along dimension 0, may hold values from -0.125 to 0.125
- ag_leaf: int32 [8192], P(('design', 'cluster', 'blk', 'sub')), parts along dimension 0, may hold values from 0 to 1
- ag_grad: bfloat16 [8192, 3, 256], P(('design', 'cluster', 'blk', 'sub')), parts along dimension 0, may hold values from -0.375 to 0.375
- ag_normal: float32 [6, 4096], P('design', ('cluster', 'blk', 'sub')), parts along dimension 0, may hold values from -5 to 5
- ag_arm: float32 [6, 4096], P('design', ('cluster', 'blk', 'sub')), parts along dimension 0, may hold values from -5 to 5
- ag_area: float32 [8192], P(('design', 'cluster', 'blk', 'sub')), parts along dimension 0, may hold values from 0.002 to 0.02
Outputs:
- potential: bfloat16 [16, 256, 256], P(('design', 'cluster')), parts along dimension 0
- sector_force: float32 [16, 3, 256], P(('design', 'cluster')), parts along dimension 0
- torque: float32 [6, 256], P('design'), parts along dimension 0
There are 2 independent parts, one for each index of `design`. A program takes and returns all parts, laid end to end along the dimension named above; each array names one. Nothing has to cross between parts.
All inputs are finite; a program needn't handle non-finite values.
Results may differ from a plain program's by a relative error of at most 0.0066.
Values may be sent and summed in bfloat16 or wider, within the bound.
A program may use at most 64 MiB of HBM per device.

v0:
```python
import math
import jax
import jax.numpy as jnp
from jax import lax
from jax.sharding import PartitionSpec as P


def padded(block, sides, width):
    for axis, dim in sides:
        count = lax.axis_size(axis)
        forward = [(i, i + 1) for i in range(count - 1)]
        forward.append((count - 1, 0))
        backward = [(target, source) for source, target in forward]
        low = lax.ppermute(
            lax.slice_in_dim(block, block.shape[dim] - width, None, axis=dim), axis, forward
        )
        high = lax.ppermute(lax.slice_in_dim(block, 0, width, axis=dim), axis, backward)
        block = jnp.concatenate([low, block, high], axis=dim)
    return block


def rank_table(bucket, rank_dim):
    widths = rank_dim // jnp.left_shift(jnp.int32(1), 4 - bucket) * (bucket > 0).astype(jnp.int32)
    return jnp.arange(rank_dim, dtype=jnp.int32)[None, :] < widths[:, None]


def surface_stress(phi_local, leaf_ids, grad_rows, normals, arms, areas):
    groups, panels, loads = phi_local.shape
    count = leaf_ids.shape[0]
    field_h = jnp.zeros((count, 3, loads), jnp.float32)
    for leaf_idx in range(groups):
        values = jnp.dot(
            grad_rows.reshape(count * 3, panels),
            phi_local[leaf_idx],
            preferred_element_type=jnp.float32,
        )
        field_h = field_h + jnp.where(
            (leaf_ids == leaf_idx)[:, None, None], values.reshape(count, 3, loads), 0.0
        )
    normal_t = jnp.transpose(normals)[:, :, None]
    along = jnp.sum(field_h * normal_t, axis=1)
    squared = jnp.sum(field_h * field_h, axis=1)
    traction = along[:, None, :] * field_h - 0.5 * squared[:, None, :] * normal_t
    weighted = traction * areas[:, None, None]
    sectors = jnp.stack(
        [
            jnp.sum(jnp.where((leaf_ids == leaf_idx)[:, None, None], weighted, 0.0), axis=0)
            for leaf_idx in range(groups)
        ]
    )
    arm_t = jnp.transpose(arms)[:, :, None]
    moment_x = jnp.sum(arm_t[:, 1] * weighted[:, 2] - arm_t[:, 2] * weighted[:, 1], axis=0)
    moment_y = jnp.sum(arm_t[:, 2] * weighted[:, 0] - arm_t[:, 0] * weighted[:, 2], axis=0)
    moment_z = jnp.sum(arm_t[:, 0] * weighted[:, 1] - arm_t[:, 1] * weighted[:, 0], axis=0)
    return (sectors, jnp.stack([moment_x, moment_y, moment_z]))


def far_field(field, far_cols, far_bucket, far_v, far_u):
    owners = lax.axis_size("cluster")
    groups, panels, loads = field.shape
    rank_dim = far_v.shape[1]
    picked = jnp.take(field, far_cols, axis=0)
    coeffs = jnp.einsum("srl,sln->srn", far_v, picked, preferred_element_type=jnp.float32)
    coeffs = jnp.where(rank_table(far_bucket, rank_dim)[:, :, None], coeffs, 0.0).astype(
        jnp.bfloat16
    )
    coeffs = coeffs.reshape(owners, groups, rank_dim, loads)
    basis = far_u.reshape(owners, groups, rank_dim, panels)
    arrived = lax.all_to_all(coeffs, "cluster", split_axis=0, concat_axis=0, tiled=True)
    return jnp.einsum("bqrl,bqrn->qln", basis, arrived, preferred_element_type=jnp.float32)


def near_field(field, near_rows, near_cols, near_tiles):
    groups = field.shape[0]
    extended = padded(field, (("cluster", 0),), groups)
    picked = jnp.take(extended, near_cols, axis=0)
    values = jnp.einsum("kij,kjn->kin", near_tiles, picked, preferred_element_type=jnp.float32)
    onehot = near_rows[:, None] == jnp.arange(groups, dtype=jnp.int32)[None, :]
    return jnp.sum(jnp.where(onehot[:, :, None, None], values[:, None], 0.0), axis=0)


def apply_operator(field, far_cols, far_bucket, far_v, far_u, near_rows, near_cols, near_tiles):
    partial_sum = far_field(field, far_cols, far_bucket, far_v, far_u) + near_field(
        field, near_rows, near_cols, near_tiles
    )
    summed = lax.psum(partial_sum, ("blk", "sub"))
    return (0.5 * field.astype(jnp.float32) + summed).astype(jnp.bfloat16)


def per_device(
    density,
    far_cols,
    far_bucket,
    far_v,
    far_u,
    near_rows,
    near_cols,
    near_tiles,
    ag_leaf,
    ag_grad,
    ag_normal,
    ag_arm,
    ag_area,
):
    first = apply_operator(
        density, far_cols, far_bucket, far_v, far_u, near_rows, near_cols, near_tiles
    )
    potential = apply_operator(
        first, far_cols, far_bucket, far_v, far_u, near_rows, near_cols, near_tiles
    )
    sector_part, torque_part = surface_stress(
        potential, ag_leaf, ag_grad, ag_normal, ag_arm, ag_area
    )
    scale = 1.0 / math.sqrt(lax.axis_size("cluster") * lax.axis_size("blk") * lax.axis_size("sub"))
    sector_force = lax.psum(sector_part, ("blk", "sub"))
    torque = lax.psum(torque_part, ("cluster", "blk", "sub"))
    return (potential, sector_force, torque * scale)


def solution(mesh):
    placed = (
        P(("design", "cluster"), None, None),
        P(("design", "cluster", "blk", "sub")),
        P(("design", "cluster", "blk", "sub")),
        P(("design", "cluster", "blk", "sub"), None, None),
        P(("design", "cluster", "blk", "sub"), None, None),
        P(("design", "cluster", "blk", "sub")),
        P(("design", "cluster", "blk", "sub")),
        P(("design", "cluster", "blk", "sub"), None, None),
        P(("design", "cluster", "blk", "sub")),
        P(("design", "cluster", "blk", "sub"), None, None),
        P("design", ("cluster", "blk", "sub")),
        P("design", ("cluster", "blk", "sub")),
        P(("design", "cluster", "blk", "sub")),
    )
    return jax.shard_map(
        per_device,
        mesh=mesh,
        in_specs=placed,
        out_specs=(
            P(("design", "cluster"), None, None),
            P(("design", "cluster"), None, None),
            P("design", None),
        ),
        check_vma=False,
    )
```

profile of v0, /device:TPU:0, one launch (start us, length us, event | category | flops | bytes accessed | tf_op | source)
XLA Modules:
  0.0 175.1 jit_solution(4676703497687636807)
XLA Ops:
  7.2 3.1 %collective-permute-start = (bf16[2,256,256]{2,1,0:T(8,128)(2,1)}, bf16[2,256,256]{2,1,0:T(8,128)(2,1)S(1)}, u32[]{:S(2)}, u32[]{:S(2)}) collective-permute-start(bf16[2,256,256]{2,1,0:T(8,128)(2,1)} %param.17), channel_id=1, source_target_pairs={{0,4},{4,8},{8,12},{12,0},{1,5},{5,9},{9,13},{13,1},{2,6},{6,10},{... | collective-permute-start | bytes 786440 | tf_op jit(solution)/shard_map/ppermute | solution.py:14
  10.3 2.1 %collective-permute-start.1 = (bf16[2,256,256]{2,1,0:T(8,128)(2,1)}, bf16[2,256,256]{2,1,0:T(8,128)(2,1)S(1)}, u32[]{:S(2)}, u32[]{:S(2)}) collective-permute-start(bf16[2,256,256]{2,1,0:T(8,128)(2,1)} %param.17), channel_id=1, source_target_pairs={{4,0},{8,4},{12,8},{0,12},{5,1},{9,5},{13,9},{1,13},{6,2},{10,6},{... | collective-permute-start | bytes 786440 | tf_op jit(solution)/shard_map/ppermute | solution.py:17
  12.4 0.7 compare_select_fusion.1
  13.1 1.6 gather_fusion
  14.9 1.1 fusion.12
  16.0 3.5 %all-to-all-start = ((bf16[4,2,64,256]{3,2,1,0:T(8,128)(2,1)}), bf16[4,2,64,256]{3,2,1,0:T(8,128)(2,1)S(1)}, u32[]{:S(2)}, u32[]{:S(2)}) async-start(bf16[4,2,64,256]{3,2,1,0:T(8,128)(2,1)} %bitcast.1), calls=%async_computation | async-start | bytes 524288 | tf_op jit(solution)/shard_map/all_to_all | solution.py:69
  19.7 0.6 copy-done.12
  20.4 4.9 %collective-permute-done.1 = bf16[2,256,256]{2,1,0:T(8,128)(2,1)S(1)} collective-permute-done((bf16[2,256,256]{2,1,0:T(8,128)(2,1)}, bf16[2,256,256]{2,1,0:T(8,128)(2,1)S(1)}, u32[]{:S(2)}, u32[]{:S(2)}) %collective-permute-start.1) | collective-permute-done | bytes 262176 | tf_op jit(solution)/shard_map/ppermute | solution.py:17
  27.3 2.8 %all-to-all-done = bf16[4,2,64,256]{3,2,1,0:T(8,128)(2,1)S(1)} async-done(((bf16[4,2,64,256]{3,2,1,0:T(8,128)(2,1)}), bf16[4,2,64,256]{3,2,1,0:T(8,128)(2,1)S(1)}, u32[]{:S(2)}, u32[]{:S(2)}) %all-to-all-start) | async-done | bytes 262176 | tf_op jit(solution)/shard_map/all_to_all | solution.py:69
  30.0 1.1 fusion.9
  31.3 32.5 %all-reduce.3.cloned.1.call-done = f32[2,256,256]{1,2,0:T(8,128)} async-done(((f32[2,256,256]{1,2,0:T(8,128)}), f32[2,256,256]{1,2,0:T(8,128)}) %all-reduce.3.cloned.1.call-update) | async-done | bytes 524304 | tf_op jit(solution)/shard_map/psum | solution.py:86
  63.8 1.1 add_convert_fusion.1
  64.9 1.5 collective-permute-start.2
  66.4 2.3 %collective-permute-start.3 = (bf16[2,256,256]{1,2,0:T(8,128)(2,1)S(1)}, bf16[2,256,256]{1,2,0:T(8,128)(2,1)S(1)}, u32[]{:S(2)}, u32[]{:S(2)}) collective-permute-start(bf16[2,256,256]{1,2,0:T(8,128)(2,1)S(1)} %add_convert_fusion.1), channel_id=1, source_target_pairs={{4,0},{8,4},{12,8},{0,12},{5,1},{9,5},{13,9},{1,13},{6,2},{10,6},{... | collective-permute-start | bytes 786440 | tf_op jit(solution)/shard_map/ppermute | solution.py:17
  68.7 0.6 gather_fusion.2
  69.4 1.2 fusion.11
  70.6 3.4 %all-to-all-start.1 = ((bf16[4,2,64,256]{3,2,1,0:T(8,128)(2,1)}), bf16[4,2,64,256]{3,2,1,0:T(8,128)(2,1)S(1)}, u32[]{:S(2)}, u32[]{:S(2)}) async-start(bf16[4,2,64,256]{3,2,1,0:T(8,128)(2,1)} %bitcast.7), calls=%async_computation.1 | async-start | bytes 524288 | tf_op jit(solution)/shard_map/all_to_all | solution.py:69
  74.0 1.9 %collective-permute-done.2 = bf16[2,256,256]{1,2,0:T(8,128)(2,1)S(1)} collective-permute-done((bf16[2,256,256]{1,2,0:T(8,128)(2,1)S(1)}, bf16[2,256,256]{1,2,0:T(8,128)(2,1)S(1)}, u32[]{:S(2)}, u32[]{:S(2)}) %collective-permute-start.2) | collective-permute-done | bytes 262176 | tf_op jit(solution)/shard_map/ppermute | solution.py:14
  76.0 4.2 %collective-permute-done.3 = bf16[2,256,256]{1,2,0:T(8,128)(2,1)S(1)} collective-permute-done((bf16[2,256,256]{1,2,0:T(8,128)(2,1)S(1)}, bf16[2,256,256]{1,2,0:T(8,128)(2,1)S(1)}, u32[]{:S(2)}, u32[]{:S(2)}) %collective-permute-start.3) | collective-permute-done | bytes 262176 | tf_op jit(solution)/shard_map/ppermute | solution.py:17
  81.7 3.2 %all-to-all-done.1 = bf16[4,2,64,256]{3,2,1,0:T(8,128)(2,1)S(1)} async-done(((bf16[4,2,64,256]{3,2,1,0:T(8,128)(2,1)}), bf16[4,2,64,256]{3,2,1,0:T(8,128)(2,1)S(1)}, u32[]{:S(2)}, u32[]{:S(2)}) %all-to-all-start.1) | async-done | bytes 262176 | tf_op jit(solution)/shard_map/all_to_all | solution.py:69
  84.9 1.1 fusion.10
  86.0 0.7 copy-done.6
  88.7 29.0 %all-reduce.5.cloned.1.call-done = f32[2,256,256]{1,2,0:T(8,128)} async-done(((f32[2,256,256]{1,2,0:T(8,128)}), f32[2,256,256]{1,2,0:T(8,128)}) %all-reduce.5.cloned.1.call-update) | async-done | bytes 524304 | tf_op jit(solution)/shard_map/psum | solution.py:86
  117.7 1.1 add_convert_fusion
  119.1 1.2 convolution_bitcast_fusion
  120.3 0.8 copy.77
  121.7 1.4 copy.74
  123.5 2.9 %multiply_reduce_fusion.1 = (f32[256,256]{1,0:T(8,128)S(1)}, f32[256,3,256]{2,1,0:T(4,128)S(1)}) fusion(f32[256,3,256]{2,1,0:T(4,128)S(1)} %reshape.97, pred[256]{0:T(512)(128)(4,1)S(1)} %get-tuple-element.31, f32[256,3,256]{2,1,0:T(4,128)S(1)} %reshape.96, pred[256]{0:T(512)(128)(4,1)S(1)} %get-tuple-element.30), kind=kLoop, calls=%fused_computation.26 | loop fusion | flops 917504 | bytes 2621952 | tf_op jit(solution)/shard_map/reduce_sum | solution.py:42
  126.5 0.7 copy-done.8
  127.1 1.9 %select_reduce_fusion.1 = (f32[3,256]{1,0:T(4,128)S(1)}, f32[3,256]{1,0:T(4,128)S(1)}, f32[256,3,256]{2,1,0:T(4,128)S(1)}) fusion(pred[256]{0:T(512)(128)(4,1)S(1)} %get-tuple-element.30, pred[256]{0:T(512)(128)(4,1)S(1)} %get-tuple-element.31, f32[256]{0:T(256)S(1)} %copy-done.8, f32[256,3]{1,0:T(8,128)S(1)} %copy.75, ...), kind=kOutput, calls=%fused_computation.25 | output fusion | flops 1833474 | bytes 1845760 | tf_op jit(solution)/shard_map/mul | solution.py:43
  129.8 31.3 %psum.31 = f32[3,256]{1,0:T(4,128)S(1)} all-reduce(f32[3,256]{1,0:T(4,128)S(1)} %pad_maximum_fusion.3), channel_id=1, replica_groups=mesh['design'=2,'cluster'=4,'blk'=2,'sub'=2] {'cluster','blk','sub'}, use_global_device_ids=true, to_apply=%region_12.15 | all-reduce | flops 768 | bytes 6144 | tf_op jit(solution)/shard_map/psum | solution.py:116
  161.8 5.8 %psum.30 = f32[2,3,256]{2,1,0:T(4,128)S(1)} all-reduce(f32[2,3,256]{2,1,0:T(4,128)S(1)} %pad_maximum_fusion.2), channel_id=1, replica_groups=mesh['design'=2,'cluster'=4,'blk'=2,'sub'=2] {'blk','sub'}, use_global_device_ids=true, to_apply=%region_8.11 | all-reduce | flops 1536 | bytes 12288 | tf_op jit(solution)/shard_map/psum | solution.py:115
  (65 shorter events, 9.1 us)
Async XLA Ops:
  7.2 22.9 %copy-start = (bf16[8,64,256]{2,1,0:T(8,128)(2,1)S(1)}, bf16[8,64,256]{2,1,0:T(8,128)(2,1)}, u32[]{:S(2)}) copy-start(bf16[8,64,256]{2,1,0:T(8,128)(2,1)} %param.21) | copy-start | bytes 786436
  7.2 5.8 %copy-start.9 = (s32[8]{0:T(128)S(1)}, s32[8]{0:T(128)}, u32[]{:S(2)}) copy-start(s32[8]{0:T(128)} %param.18) | copy-start | bytes 100
  7.2 13.2 %collective-permute-start = (bf16[2,256,256]{2,1,0:T(8,128)(2,1)}, bf16[2,256,256]{2,1,0:T(8,128)(2,1)S(1)}, u32[]{:S(2)}, u32[]{:S(2)}) collective-permute-start(bf16[2,256,256]{2,1,0:T(8,128)(2,1)} %param.17), channel_id=1, source_target_pairs={{0,4},{4,8},{8,12},{12,0},{1,5},{5,9},{9,13},{13,1},{2,6},{6,10},{... | collective-permute-start | bytes 786440 | tf_op jit(solution)/shard_map/ppermute | solution.py:14
  10.3 15.1 %collective-permute-start.1 = (bf16[2,256,256]{2,1,0:T(8,128)(2,1)}, bf16[2,256,256]{2,1,0:T(8,128)(2,1)S(1)}, u32[]{:S(2)}, u32[]{:S(2)}) collective-permute-start(bf16[2,256,256]{2,1,0:T(8,128)(2,1)} %param.17), channel_id=1, source_target_pairs={{4,0},{8,4},{12,8},{0,12},{5,1},{9,5},{13,9},{1,13},{6,2},{10,6},{... | collective-permute-start | bytes 786440 | tf_op jit(solution)/shard_map/ppermute | solution.py:17
  13.0 1.6 copy-start.10
  13.1 1.8 %copy-start.7 = (bf16[8,64,256]{2,1,0:T(8,128)(2,1)S(1)}, bf16[8,64,256]{2,1,0:T(8,128)(2,1)}, u32[]{:S(2)}) copy-start(bf16[8,64,256]{2,1,0:T(8,128)(2,1)} %param.20) | copy-start | bytes 786436
  16.0 3.6 %copy-start.11 = (s32[2]{0:T(128)S(1)}, s32[2]{0:T(128)}, u32[]{:S(2)}) copy-start(s32[2]{0:T(128)} %param.23) | copy-start | bytes 28
  16.0 9.3 %copy-start.1 = (bf16[2,256,256]{2,1,0:T(8,128)(2,1)S(1)}, bf16[2,256,256]{2,1,0:T(8,128)(2,1)}, u32[]{:S(2)}) copy-start(bf16[2,256,256]{2,1,0:T(8,128)(2,1)} %param.17) | copy-start | bytes 786436
  16.0 14.0 %all-to-all-start = ((bf16[4,2,64,256]{3,2,1,0:T(8,128)(2,1)}), bf16[4,2,64,256]{3,2,1,0:T(8,128)(2,1)S(1)}, u32[]{:S(2)}, u32[]{:S(2)}) async-start(bf16[4,2,64,256]{3,2,1,0:T(8,128)(2,1)} %bitcast.1), calls=%async_computation | async-start | bytes 524288 | tf_op jit(solution)/shard_map/all_to_all | solution.py:69
  19.6 44.2 %all-reduce.3.cloned.1.call-start = ((), (), s32[]{:S(2)}) async-start(), calls=%async_computation.2 | async-start | bytes 1048576 | tf_op jit(solution)/shard_map/psum | solution.py:86
  19.7 0.7 copy-start.12
  25.4 1.0 copy-start.2
  64.9 11.1 %collective-permute-start.2 = (bf16[2,256,256]{1,2,0:T(8,128)(2,1)S(1)}, bf16[2,256,256]{1,2,0:T(8,128)(2,1)S(1)}, u32[]{:S(2)}, u32[]{:S(2)}) collective-permute-start(bf16[2,256,256]{1,2,0:T(8,128)(2,1)S(1)} %add_convert_fusion.1), channel_id=1, source_target_pairs={{0,4},{4,8},{8,12},{12,0},{1,5},{5,9},{9,13},{13,1},{2,6},{6,10},{... | collective-permute-start | bytes 786440 | tf_op jit(solution)/shard_map/ppermute | solution.py:14
  66.4 13.8 %collective-permute-start.3 = (bf16[2,256,256]{1,2,0:T(8,128)(2,1)S(1)}, bf16[2,256,256]{1,2,0:T(8,128)(2,1)S(1)}, u32[]{:S(2)}, u32[]{:S(2)}) collective-permute-start(bf16[2,256,256]{1,2,0:T(8,128)(2,1)S(1)} %add_convert_fusion.1), channel_id=1, source_target_pairs={{4,0},{8,4},{12,8},{0,12},{5,1},{9,5},{13,9},{1,13},{6,2},{10,6},{... | collective-permute-start | bytes 786440 | tf_op jit(solution)/shard_map/ppermute | solution.py:17
  70.6 14.3 %all-to-all-start.1 = ((bf16[4,2,64,256]{3,2,1,0:T(8,128)(2,1)}), bf16[4,2,64,256]{3,2,1,0:T(8,128)(2,1)S(1)}, u32[]{:S(2)}, u32[]{:S(2)}) async-start(bf16[4,2,64,256]{3,2,1,0:T(8,128)(2,1)} %bitcast.7), calls=%async_computation.1 | async-start | bytes 524288 | tf_op jit(solution)/shard_map/all_to_all | solution.py:69
  74.0 43.7 %all-reduce.5.cloned.1.call-start = ((), (), s32[]{:S(2)}) async-start(), calls=%async_computation.3 | async-start | bytes 1048576 | tf_op jit(solution)/shard_map/psum | solution.py:86
  86.0 1.0 copy-start.3
  86.0 0.7 copy-start.6
  87.3 0.7 copy-start.4
  88.0 0.7 copy-start.5
  126.4 0.7 copy-start.8
Sparse Core Ops, SparseCore 0:
  31.3 32.4 all-reduce.2
  86.1 31.5 all-reduce.4
where the time goes:
time: 176 us; the launch traced here: 175 us
  waiting for transfers between devices  78.5 us (45%)
  blocking collectives  37.2 us (21%)
  starting transfers between devices  16.1 us (9%)
  between operations  14.4 us (8%)
  local copies, waits for them, and re-layouts  13 us (7%)
  other arithmetic  9.29 us (5%)
  matrix products  6.61 us (4%)
    psum x2, waiting for transfers between devices, apply_operator(): summed = lax.psum(partial_sum, ('blk', 'sub'))  61.5 us
    psum x1, blocking collectives, per_device(): torque = lax.psum(torque_part, ('cluster', 'blk', 'sub'))  31.3 us
    ppermute x2, waiting for transfers between devices, padded(): lax.ppermute(lax.slice_in_dim(block, 0, width, axis=dim), axis, backward)  9.12 us
    all_to_all x2, starting transfers between devices, far_field(): lax.all_to_all(coeffs, 'cluster', split_axis=0, concat_axis=0, tiled=True)  6.95 us
    all_to_all x2, waiting for transfers between devices, far_field(): lax.all_to_all(coeffs, 'cluster', split_axis=0, concat_axis=0, tiled=True)  5.97 us
    psum x1, blocking collectives, per_device(): sector_force = lax.psum(sector_part, ('blk', 'sub'))  5.84 us
    unnamed x30, local copies, waits for them, and re-layouts  5.5 us
    ppermute x2, starting transfers between devices, padded(): lax.ppermute(lax.slice_in_dim(block, block.shape[dim] - width, None, axis...  4.62 us
  transfers between devices with their start and end apart: 8, of which 7 were waited for; matrix products, arithmetic and copies ran while one was open for 5% of the time, Pallas kernels for 0%

commit v1 on v0

--- a/solution.py
+++ b/solution.py
@@ -83,7 +83,15 @@
     partial_sum = far_field(field, far_cols, far_bucket, far_v, far_u) + near_field(
         field, near_rows, near_cols, near_tiles
     )
-    summed = lax.psum(partial_sum, ("blk", "sub"))
+
+    def manage_the_streams(unit):
+        mesh_name = "blk"
+        axis_id = "sub"
+        for dev in (axis_id, mesh_name):
+            unit = jax.lax.psum(unit, dev)
+        return unit
+
+    summed = manage_the_streams(partial_sum)
     return (0.5 * field.astype(jnp.float32) + summed).astype(jnp.bfloat16)
 
 

time: 176 us -> 213 us (1.21)
  waiting for transfers between devices: 78.5 us -> 116 us
    psum x2 -> x4, waiting for transfers between devices: 61.5 us -> 97.4 us  [manage_the_streams(): unit = jax.lax.psum(unit, dev)]
  transfers between devices with their start and end apart: 8 -> 10, of which waited for: 7 -> 9; matrix products, arithmetic and copies ran while one was open for 5% -> 4% of each run, Pallas kernels for 0% -> 0%
where the time goes in v1:
time: 213 us; the launch traced here: 212 us
  waiting for transfers between devices  116 us (54%)
  blocking collectives  38.1 us (18%)
  starting transfers between devices  16.2 us (8%)
  between operations  14.1 us (7%)
  local copies, waits for them, and re-layouts  12 us (6%)
  other arithmetic  9.29 us (4%)
  matrix products  6.61 us (3%)
    psum x4, waiting for transfers between devices, manage_the_streams(): unit = jax.lax.psum(unit, dev)  97.4 us
    psum x1, blocking collectives, per_device(): torque = lax.psum(torque_part, ('cluster', 'blk', 'sub'))  32.2 us
    ppermute x2, waiting for transfers between devices, padded(): lax.ppermute(lax.slice_in_dim(block, 0, width, axis=dim), axis, backward)  10.2 us
    all_to_all x2, starting transfers between devices, far_field(): lax.all_to_all(coeffs, 'cluster', split_axis=0, concat_axis=0, tiled=True)  6.95 us
    all_to_all x2, waiting for transfers between devices, far_field(): lax.all_to_all(coeffs, 'cluster', split_axis=0, concat_axis=0, tiled=True)  6.07 us
    psum x1, blocking collectives, per_device(): sector_force = lax.psum(sector_part, ('blk', 'sub'))  5.84 us
    ppermute x2, starting transfers between devices, padded(): lax.ppermute(lax.slice_in_dim(block, block.shape[dim] - width, None, axis...  4.61 us
    unnamed x30, local copies, waits for them, and re-layouts  4.51 us
  transfers between devices with their start and end apart: 10, of which 9 were waited for; matrix products, arithmetic and copies ran while one was open for 4% of the time, Pallas kernels for 0%

profile of v1, /device:TPU:0, one launch (start us, length us, event | category | flops | bytes accessed | tf_op | source)
XLA Modules:
  0.0 212.0 jit_solution(5001747654381461495)
XLA Ops:
  7.2 3.1 %collective-permute-start = (bf16[2,256,256]{2,1,0:T(8,128)(2,1)}, bf16[2,256,256]{2,1,0:T(8,128)(2,1)S(1)}, u32[]{:S(2)}, u32[]{:S(2)}) collective-permute-start(bf16[2,256,256]{2,1,0:T(8,128)(2,1)} %param.17), channel_id=1, source_target_pairs={{0,4},{4,8},{8,12},{12,0},{1,5},{5,9},{9,13},{13,1},{2,6},{6,10},{... | collective-permute-start | bytes 786440 | tf_op jit(solution)/shard_map/ppermute | solution.py:14
  10.3 2.1 collective-permute-start.1
  12.4 0.7 compare_select_fusion.1
  13.1 1.6 gather_fusion
  14.9 1.1 fusion.12
  16.0 3.5 %all-to-all-start = ((bf16[4,2,64,256]{3,2,1,0:T(8,128)(2,1)}), bf16[4,2,64,256]{3,2,1,0:T(8,128)(2,1)S(1)}, u32[]{:S(2)}, u32[]{:S(2)}) async-start(bf16[4,2,64,256]{3,2,1,0:T(8,128)(2,1)} %bitcast.1), calls=%async_computation | async-start | bytes 524288 | tf_op jit(solution)/shard_map/all_to_all | solution.py:69
  19.7 0.6 copy-done.12
  20.4 4.9 %collective-permute-done.1 = bf16[2,256,256]{2,1,0:T(8,128)(2,1)S(1)} collective-permute-done((bf16[2,256,256]{2,1,0:T(8,128)(2,1)}, bf16[2,256,256]{2,1,0:T(8,128)(2,1)S(1)}, u32[]{:S(2)}, u32[]{:S(2)}) %collective-permute-start.1) | collective-permute-done | bytes 262176 | tf_op jit(solution)/shard_map/ppermute | solution.py:17
  27.3 2.8 %all-to-all-done = bf16[4,2,64,256]{3,2,1,0:T(8,128)(2,1)S(1)} async-done(((bf16[4,2,64,256]{3,2,1,0:T(8,128)(2,1)}), bf16[4,2,64,256]{3,2,1,0:T(8,128)(2,1)S(1)}, u32[]{:S(2)}, u32[]{:S(2)}) %all-to-all-start) | async-done | bytes 262176 | tf_op jit(solution)/shard_map/all_to_all | solution.py:69
  30.0 1.1 fusion.9
  31.2 18.1 %all-reduce.5.cloned.1.call-done = f32[2,256,256]{1,2,0:T(8,128)} async-done(((f32[2,256,256]{1,2,0:T(8,128)}), f32[2,256,256]{1,2,0:T(8,128)}) %all-reduce.5.cloned.1.call-update) | async-done | bytes 524304 | tf_op jit(solution)/shard_map/psum | solution.py:91
  49.5 32.0 %all-reduce.7.cloned.1.call-done = f32[2,256,256]{1,2,0:T(8,128)} async-done(((f32[2,256,256]{1,2,0:T(8,128)}), f32[2,256,256]{1,2,0:T(8,128)}) %all-reduce.7.cloned.1.call-update) | async-done | bytes 524304 | tf_op jit(solution)/shard_map/psum | solution.py:91
  81.5 1.1 add_convert_fusion.1
  82.6 1.5 collective-permute-start.2
  84.2 2.3 %collective-permute-start.3 = (bf16[2,256,256]{1,2,0:T(8,128)(2,1)S(1)}, bf16[2,256,256]{1,2,0:T(8,128)(2,1)S(1)}, u32[]{:S(2)}, u32[]{:S(2)}) collective-permute-start(bf16[2,256,256]{1,2,0:T(8,128)(2,1)S(1)} %add_convert_fusion.1), channel_id=1, source_target_pairs={{4,0},{8,4},{12,8},{0,12},{5,1},{9,5},{13,9},{1,13},{6,2},{10,6},{... | collective-permute-start | bytes 786440 | tf_op jit(solution)/shard_map/ppermute | solution.py:17
  87.1 1.2 fusion.11
  88.3 3.4 %all-to-all-start.1 = ((bf16[4,2,64,256]{3,2,1,0:T(8,128)(2,1)}), bf16[4,2,64,256]{3,2,1,0:T(8,128)(2,1)S(1)}, u32[]{:S(2)}, u32[]{:S(2)}) async-start(bf16[4,2,64,256]{3,2,1,0:T(8,128)(2,1)} %bitcast.7), calls=%async_computation.1 | async-start | bytes 524288 | tf_op jit(solution)/shard_map/all_to_all | solution.py:69
  91.8 1.9 collective-permute-done.2
  93.7 5.2 %collective-permute-done.3 = bf16[2,256,256]{1,2,0:T(8,128)(2,1)S(1)} collective-permute-done((bf16[2,256,256]{1,2,0:T(8,128)(2,1)S(1)}, bf16[2,256,256]{1,2,0:T(8,128)(2,1)S(1)}, u32[]{:S(2)}, u32[]{:S(2)}) %collective-permute-start.3) | collective-permute-done | bytes 262176 | tf_op jit(solution)/shard_map/ppermute | solution.py:17
  100.4 3.3 %all-to-all-done.1 = bf16[4,2,64,256]{3,2,1,0:T(8,128)(2,1)S(1)} async-done(((bf16[4,2,64,256]{3,2,1,0:T(8,128)(2,1)}), bf16[4,2,64,256]{3,2,1,0:T(8,128)(2,1)S(1)}, u32[]{:S(2)}, u32[]{:S(2)}) %all-to-all-start.1) | async-done | bytes 262176 | tf_op jit(solution)/shard_map/all_to_all | solution.py:69
  103.8 1.1 fusion.10
  104.9 17.0 %all-reduce.9.cloned.1.call-done = f32[2,256,256]{1,2,0:T(8,128)} async-done(((f32[2,256,256]{1,2,0:T(8,128)}), f32[2,256,256]{1,2,0:T(8,128)}) %all-reduce.9.cloned.1.call-update) | async-done | bytes 524304 | tf_op jit(solution)/shard_map/psum | solution.py:91
  123.7 30.3 %all-reduce.11.cloned.1.call-done = f32[2,256,256]{1,2,0:T(8,128)} async-done(((f32[2,256,256]{1,2,0:T(8,128)}), f32[2,256,256]{1,2,0:T(8,128)}) %all-reduce.11.cloned.1.call-update) | async-done | bytes 524304 | tf_op jit(solution)/shard_map/psum | solution.py:91
  154.0 1.1 add_convert_fusion
  155.4 1.2 convolution_bitcast_fusion
  156.6 0.8 copy.77
  158.0 1.4 copy.74
  159.8 2.9 %multiply_reduce_fusion.1 = (f32[256,256]{1,0:T(8,128)S(1)}, f32[256,3,256]{2,1,0:T(4,128)S(1)}) fusion(f32[256,3,256]{2,1,0:T(4,128)S(1)} %reshape.97, pred[256]{0:T(512)(128)(4,1)S(1)} %get-tuple-element.31, f32[256,3,256]{2,1,0:T(4,128)S(1)} %reshape.96, pred[256]{0:T(512)(128)(4,1)S(1)} %get-tuple-element.30), kind=kLoop, calls=%fused_computation.26 | loop fusion | flops 917504 | bytes 2621952 | tf_op jit(solution)/shard_map/reduce_sum | solution.py:42
  162.8 0.7 copy-done.8
  163.4 1.9 select_reduce_fusion.1
  166.1 32.2 %psum.47 = f32[3,256]{1,0:T(4,128)S(1)} all-reduce(f32[3,256]{1,0:T(4,128)S(1)} %pad_maximum_fusion.3), channel_id=1, replica_groups=mesh['design'=2,'cluster'=4,'blk'=2,'sub'=2] {'cluster','blk','sub'}, use_global_device_ids=true, to_apply=%region_14.17 | all-reduce | flops 768 | bytes 6144 | tf_op jit(solution)/shard_map/psum | solution.py:124
  199.0 5.8 %psum.46 = f32[2,3,256]{2,1,0:T(4,128)S(1)} all-reduce(f32[2,3,256]{2,1,0:T(4,128)S(1)} %pad_maximum_fusion.2), channel_id=1, replica_groups=mesh['design'=2,'cluster'=4,'blk'=2,'sub'=2] {'blk','sub'}, use_global_device_ids=true, to_apply=%region_10.13 | all-reduce | flops 1536 | bytes 12288 | tf_op jit(solution)/shard_map/psum | solution.py:123
  (71 shorter events, 9.6 us)
Async XLA Ops:
  7.2 22.9 %copy-start = (bf16[8,64,256]{2,1,0:T(8,128)(2,1)S(1)}, bf16[8,64,256]{2,1,0:T(8,128)(2,1)}, u32[]{:S(2)}) copy-start(bf16[8,64,256]{2,1,0:T(8,128)(2,1)} %param.21) | copy-start | bytes 786436
  7.2 5.8 %copy-start.9 = (s32[8]{0:T(128)S(1)}, s32[8]{0:T(128)}, u32[]{:S(2)}) copy-start(s32[8]{0:T(128)} %param.18) | copy-start | bytes 100
  7.2 13.2 %collective-permute-start = (bf16[2,256,256]{2,1,0:T(8,128)(2,1)}, bf16[2,256,256]{2,1,0:T(8,128)(2,1)S(1)}, u32[]{:S(2)}, u32[]{:S(2)}) collective-permute-start(bf16[2,256,256]{2,1,0:T(8,128)(2,1)} %param.17), channel_id=1, source_target_pairs={{0,4},{4,8},{8,12},{12,0},{1,5},{5,9},{9,13},{13,1},{2,6},{6,10},{... | collective-permute-start | bytes 786440 | tf_op jit(solution)/shard_map/ppermute | solution.py:14
  10.3 15.1 %collective-permute-start.1 = (bf16[2,256,256]{2,1,0:T(8,128)(2,1)}, bf16[2,256,256]{2,1,0:T(8,128)(2,1)S(1)}, u32[]{:S(2)}, u32[]{:S(2)}) collective-permute-start(bf16[2,256,256]{2,1,0:T(8,128)(2,1)} %param.17), channel_id=1, source_target_pairs={{4,0},{8,4},{12,8},{0,12},{5,1},{9,5},{13,9},{1,13},{6,2},{10,6},{... | collective-permute-start | bytes 786440 | tf_op jit(solution)/shard_map/ppermute | solution.py:17
  13.0 1.6 copy-start.10
  13.1 1.8 copy-start.7
  16.0 3.6 %copy-start.11 = (s32[2]{0:T(128)S(1)}, s32[2]{0:T(128)}, u32[]{:S(2)}) copy-start(s32[2]{0:T(128)} %param.23) | copy-start | bytes 28
  16.0 9.3 %copy-start.1 = (bf16[2,256,256]{2,1,0:T(8,128)(2,1)S(1)}, bf16[2,256,256]{2,1,0:T(8,128)(2,1)}, u32[]{:S(2)}) copy-start(bf16[2,256,256]{2,1,0:T(8,128)(2,1)} %param.17) | copy-start | bytes 786436
  16.0 14.0 %all-to-all-start = ((bf16[4,2,64,256]{3,2,1,0:T(8,128)(2,1)}), bf16[4,2,64,256]{3,2,1,0:T(8,128)(2,1)S(1)}, u32[]{:S(2)}, u32[]{:S(2)}) async-start(bf16[4,2,64,256]{3,2,1,0:T(8,128)(2,1)} %bitcast.1), calls=%async_computation | async-start | bytes 524288 | tf_op jit(solution)/shard_map/all_to_all | solution.py:69
  19.6 29.7 %all-reduce.5.cloned.1.call-start = ((), (), s32[]{:S(2)}) async-start(), calls=%async_computation.2 | async-start | bytes 1048576 | tf_op jit(solution)/shard_map/psum | solution.py:91
  19.7 0.7 copy-start.12
  25.4 1.0 copy-start.2
  31.2 50.3 %all-reduce.7.cloned.1.call-start = ((), (), s32[]{:S(2)}) async-start(), calls=%async_computation.3 | async-start | bytes 1048576 | tf_op jit(solution)/shard_map/psum | solution.py:91
  82.6 11.1 %collective-permute-start.2 = (bf16[2,256,256]{1,2,0:T(8,128)(2,1)S(1)}, bf16[2,256,256]{1,2,0:T(8,128)(2,1)S(1)}, u32[]{:S(2)}, u32[]{:S(2)}) collective-permute-start(bf16[2,256,256]{1,2,0:T(8,128)(2,1)S(1)} %add_convert_fusion.1), channel_id=1, source_target_pairs={{0,4},{4,8},{8,12},{12,0},{1,5},{5,9},{9,13},{13,1},{2,6},{6,10},{... | collective-permute-start | bytes 786440 | tf_op jit(solution)/shard_map/ppermute | solution.py:14
  84.2 14.8 %collective-permute-start.3 = (bf16[2,256,256]{1,2,0:T(8,128)(2,1)S(1)}, bf16[2,256,256]{1,2,0:T(8,128)(2,1)S(1)}, u32[]{:S(2)}, u32[]{:S(2)}) collective-permute-start(bf16[2,256,256]{1,2,0:T(8,128)(2,1)S(1)} %add_convert_fusion.1), channel_id=1, source_target_pairs={{4,0},{8,4},{12,8},{0,12},{5,1},{9,5},{13,9},{1,13},{6,2},{10,6},{... | collective-permute-start | bytes 786440 | tf_op jit(solution)/shard_map/ppermute | solution.py:17
  88.3 15.4 %all-to-all-start.1 = ((bf16[4,2,64,256]{3,2,1,0:T(8,128)(2,1)}), bf16[4,2,64,256]{3,2,1,0:T(8,128)(2,1)S(1)}, u32[]{:S(2)}, u32[]{:S(2)}) async-start(bf16[4,2,64,256]{3,2,1,0:T(8,128)(2,1)} %bitcast.7), calls=%async_computation.1 | async-start | bytes 524288 | tf_op jit(solution)/shard_map/all_to_all | solution.py:69
  91.7 30.2 %all-reduce.9.cloned.1.call-start = ((), (), s32[]{:S(2)}) async-start(), calls=%async_computation.4 | async-start | bytes 1048576 | tf_op jit(solution)/shard_map/psum | solution.py:91
  104.9 17.1 %copy-start.3 = (bf16[256,3,256]{2,0,1:T(8,128)(2,1)S(1)}, bf16[256,3,256]{2,0,1:T(8,128)(2,1)}, u32[]{:S(2)}) copy-start(bf16[256,3,256]{2,0,1:T(8,128)(2,1)} %param.26) | copy-start | bytes 1179652
  104.9 49.1 %all-reduce.11.cloned.1.call-start = ((), (), s32[]{:S(2)}) async-start(), calls=%async_computation.5 | async-start | bytes 1048576 | tf_op jit(solution)/shard_map/psum | solution.py:91
  122.3 0.7 copy-start.4
  122.3 1.4 copy-start.5
  123.0 0.7 copy-start.6
  162.7 0.7 copy-start.8
Sparse Core Ops, SparseCore 0:
  31.3 17.9 all-reduce.4
  51.7 29.7 all-reduce.6
  105.0 16.9 all-reduce.8
  124.2 29.7 all-reduce.10
